TPU v7x, 256 devices: a whole 4x4x8 slice. The times are simulated.
256 devices in a mesh: rep: 8 (over z), shard: 32 (over x, y, core).
Axes of the slice: x: 4, y: 4, z: 8, core: 2. Of those that a mesh axis runs over, the one named last changes fastest.
Arguments:
- acts: bfloat16 [131072, 2048], P(('rep', 'shard')), may hold values from -6 to 6
- cotangent: bfloat16 [131072, 5120], P(('rep', 'shard')), may hold values from -0.046875 to 0.046875
- error_prev: float32 [8, 2048, 5120], P('rep', 'shard'), may hold values from -6 to 6
- q_prev: float32 [5120, 64], replicated, may hold values from -6 to 6
Outputs:
- update: bfloat16 [2048, 5120], P('shard')
- error_next: float32 [8, 2048, 5120], P('rep', 'shard')
- q_next: float32 [5120, 64], replicated
All inputs are finite; a program needn't handle non-finite values.
Results may differ from a plain program's by a relative error of at most 0.025.
Values may be sent and summed in bfloat16 or wider, within the bound.
No kernel may reach another device: no remote copies, remote signals or barrier semaphores. Data moves between devices by JAX's collectives and lax.ppermute only.
A program may use at most 128 MiB of HBM per device.

v0:
```python
import functools

import jax
import jax.numpy as jnp
from jax import lax
from jax.experimental import pallas as pl
from jax.experimental.pallas import tpu as pltpu
from jax.sharding import Mesh, PartitionSpec as P

HI = lax.Precision.HIGHEST
SHARD = ("x", "y", "c")
f32 = jnp.float32
bf16 = jnp.bfloat16
VMEM = pl.BlockSpec(memory_space=pltpu.VMEM)
SMEM = pl.BlockSpec(memory_space=pltpu.SMEM)
HBM = pl.BlockSpec(memory_space=pl.ANY)
NT = (((1,), (1,)), ((), ()))
CHEAP = pl.CostEstimate(flops=1, bytes_accessed=1, transcendentals=0)
CHAIN = pl.CostEstimate(flops=5 * 10**10, bytes_accessed=1, transcendentals=0)
LARGE = 56 * 2**20


def terms(a, count):
    out = []
    for _ in range(count):
        top = a.astype(bf16)
        out.append(top)
        a = a - top.astype(f32)
    return out


def rows2(a):
    return jnp.concatenate(terms(a, 2), 0)


def fold(a):
    size = a.shape[0] // 2
    return a[:size] + a[size:]


def call(body, outs, ins, name, scratch=(), limit=8, cost=CHAIN):
    return pl.pallas_call(
        body,
        out_shape=outs,
        in_specs=[spec for _, spec in ins],
        out_specs=[VMEM] * len(outs),
        scratch_shapes=list(scratch),
        name=name,
        compiler_params=pltpu.CompilerParams(vmem_limit_bytes=limit * 2**20),
        cost_estimate=cost,
    )(*[a for a, _ in ins])


def shape(dims, dtype):
    return jax.ShapeDtypeStruct(dims, dtype)


def left_body(meta, q_hbm, cot_hbm, acts_hbm, err_hbm, out, q_t, cot, acts, err, t, p_t, sems):
    tokens = cot.shape[0]
    chunks = sems.shape[0] - 3
    size = tokens // chunks
    slabs = [slice(i * size, (i + 1) * size) for i in range(chunks)]
    copies = [pltpu.make_async_copy(q_hbm, q_t, sems.at[chunks])]
    copies += [
        pltpu.make_async_copy(cot_hbm.at[slab], cot.at[slab], sems.at[i])
        for i, slab in enumerate(slabs)
    ]
    copies.append(pltpu.make_async_copy(acts_hbm, acts, sems.at[chunks + 1]))
    copies.append(pltpu.make_async_copy(err_hbm, err, sems.at[chunks + 2]))
    for copy in copies:
        copy.start()
    copies[0].wait()
    q2 = rows2(q_t[...])
    for copy, slab in zip(copies[1:-2], slabs):
        copy.wait()
        t[slab] = lax.dot_general(cot[slab], q2, NT, preferred_element_type=f32)
    t2 = rows2(fold(t[...].T))
    copies[-2].wait()
    p_t[...] = fold(jnp.dot(t2, acts[...], preferred_element_type=f32))
    copies[-1].wait()
    own = fold(lax.dot_general(q2, rows2(err[...]), NT, preferred_element_type=f32))
    rows = err.shape[0]
    own = own[:, :rows] + own[:, rows:]
    s = meta[0]
    zero = jnp.zeros_like(own)
    odd = (s % 2) == 1
    own = jnp.concatenate([jnp.where(odd, zero, own), jnp.where(odd, own, zero)], 1)
    at = pl.ds(pl.multiple_of((s // 2) * (2 * rows), 2 * rows), 2 * rows)
    p_t[:, at] += own
    _, high, wide = out.shape
    across = p_t.shape[1] // wide
    for block in range(out.shape[0]):
        g, l = divmod(block, across)
        out[block] = p_t[g * high : (g + 1) * high, l * wide : (l + 1) * wide]


def left(meta, q_t, cot, acts, err, n_shard):
    rank = q_t.shape[0]
    tokens, dim = acts.shape
    high, wide = 8, rank * dim // n_shard // 8
    return call(
        left_body, [shape((n_shard, high, wide), f32)],
        [(meta, SMEM), (q_t, HBM), (cot, HBM), (acts, HBM), (err, HBM)],
        "left",
        [pltpu.VMEM(a.shape, a.dtype) for a in (q_t, cot, acts, err)]
        + [pltpu.VMEM((tokens, 2 * rank), f32), pltpu.VMEM((rank, dim), f32)]
        + [pltpu.SemaphoreType.DMA((4 + 3,))],
        limit=56,
    )[0]


def total_body(scale, part, out):
    total = part[0].astype(f32)
    for index in range(1, part.shape[0]):
        total += part[index].astype(f32)
    total = (total * scale).astype(out.dtype)
    for index in range(out.shape[0]):
        out[index] = total


def total(part, copies, dtype, name, scale=1.0, cost=CHAIN):
    out = shape((copies,) + part.shape[1:], dtype)
    return call(functools.partial(total_body, scale), [out], [(part, VMEM)], name, limit=4, cost=cost)[0]


def inverse_factor(gram):
    n = gram.shape[0]
    ident = (
        lax.broadcasted_iota(jnp.int32, (n, n), 0) == lax.broadcasted_iota(jnp.int32, (n, n), 1)
    ).astype(f32)
    work = jnp.concatenate([gram, ident], 1)
    index = lax.broadcasted_iota(jnp.int32, work.shape, 0)
    step = 4
    for k in range(0, n, step):
        here = range(step)
        row = [work[k + i : k + i + 1, :] for i in here]
        col = [jnp.broadcast_to(work[:, k + i : k + i + 1], work.shape) for i in here]
        entry = [[col[j][k + i : k + i + 1, :] for j in here] for i in here]
        inv, root = [], []
        for j in here:
            inv.append(1.0 / entry[j][j])
            guess = lax.rsqrt(entry[j][j])
            root.append(guess * (1.5 - 0.5 * entry[j][j] * guess * guess))
            for i in range(j + 1, step):
                ratio = entry[i][j] * inv[j]
                row[i] = row[i] - ratio * row[j]
                for l in range(j + 1, step):
                    entry[i][l] = entry[i][l] - ratio * entry[j][l]
            for l in range(j + 1, step):
                col[l] = col[l] - col[j] * (inv[j] * entry[j][l])
        change = col[0] * (inv[0] * row[0])
        for j in range(1, step):
            change += col[j] * (inv[j] * row[j])
        work = jnp.where(index >= k + step, work - change, work)
        for j in here:
            work = jnp.where(index == k + j, row[j] * root[j], work)
    return work[:, n:]


def right_body(meta, parts, acts_hbm, cot_hbm, err_hbm, out, own_out, p_t, acts, cot, err, sems):
    pairs = ((acts_hbm, acts), (cot_hbm, cot), (err_hbm, err))
    copies = [pltpu.make_async_copy(a, b, sems.at[i]) for i, (a, b) in enumerate(pairs)]
    for copy in copies:
        copy.start()
    _, high, wide = parts.shape
    across = p_t.shape[1] // wide
    for block in range(parts.shape[0]):
        g, l = divmod(block, across)
        p_t[g * high : (g + 1) * high, l * wide : (l + 1) * wide] = parts[block]
    rank = p_t.shape[0]
    rows = err.shape[0]
    p = p_t[...]
    p3 = jnp.concatenate(terms(p, 3), 0)
    grams = lax.dot_general(p3, p3, NT, preferred_element_type=f32)
    gram = jnp.zeros((rank, rank), f32)
    for i in reversed(range(3)):
        for j in reversed(range(3)):
            gram += grams[i * rank : (i + 1) * rank, j * rank : (j + 1) * rank]
    inverse = inverse_factor(gram)
    p_hat = jnp.dot(inverse, p, precision=HI, preferred_element_type=f32)
    p_t[...] = p_hat
    copies[0].wait()
    w = fold(lax.dot_general(rows2(p_hat), acts[...], NT, preferred_element_type=f32))
    w2 = rows2(w)
    s = meta[0]
    both = p_t[:, pl.ds(pl.multiple_of((s // 2) * (2 * rows), 2 * rows), 2 * rows)]
    own = jnp.where((s % 2) == 1, both[:, rows:], both[:, :rows])
    own_out[...] = own
    own_top, own_rest = terms(own, 2)
    own3 = jnp.concatenate([own_top, own_rest, own_top], 1)
    copies[1].wait()
    copies[2].wait()
    _, high, wide = out.shape
    across = cot.shape[1] // wide
    for l in range(across):
        cols = slice(l * wide, (l + 1) * wide)
        err_top, err_rest = terms(err[:, cols], 2)
        err3 = jnp.concatenate([err_top, err_top, err_rest], 0)
        q = fold(jnp.dot(w2, cot[:, cols], preferred_element_type=f32))
        q += jnp.dot(own3, err3, preferred_element_type=f32)
        q = q.astype(out.dtype)
        for g in range(rank // high):
            out[g * across + l] = q[g * high : (g + 1) * high]


def last_body(meta, parts, own_t, mine, theirs, err, update, error_next, q_out):
    _, high, wide = parts.shape
    rank = own_t.shape[0]
    across = err.shape[1] // wide
    own_top, own_rest = terms(own_t[...].T, 2)
    own2 = jnp.concatenate([own_top, own_rest], 1)
    c = lax.rem(meta[0], jnp.int32(2))
    for l in range(across):
        cols = slice(l * wide, (l + 1) * wide)
        q = jnp.concatenate([parts[g * across + l] for g in range(rank // high)], 0)
        q_out[:, cols] = q.astype(f32)
        full = jnp.dot(own2, jnp.concatenate([q, q], 0), preferred_element_type=f32)
        update[:, cols] = full.astype(bf16)
        side, at = divmod(l * wide, mine.shape[1])
        there = slice(at, at + wide)
        grad = jnp.where(c == side, mine[:, there].astype(f32), theirs[:, there].astype(f32))
        error_next[:, cols] = grad + err[:, cols] - full


ORDER = [(2, 0), (2, 1), (2, 2), (2, 3), (1, 2), (1, 3), (3, 0), (3, 1)]
ORDER += [(1, 0), (1, 1), (3, 2), (3, 3), (0, 0), (0, 1), (0, 2), (0, 3)]


def place_of(s, side):
    two = jnp.int32(2)
    chip = lax.div(s, two)
    return lax.rem(s, two), lax.div(chip, jnp.int32(side)), lax.rem(chip, jnp.int32(side))


def product_body(side, meta, a0, a1, y0, y1, *refs):
    outs, (a0_v, a1_v, left, right, full, sems, out_sems) = refs[:-7], refs[-7:]
    _, per, rows, cols = full.shape
    tokens = a0.shape[0]
    c, x, y = place_of(meta[0], side)
    at = pl.ds(pl.multiple_of(c * cols, 128), cols)
    copies = [
        pltpu.make_async_copy(a0, a0_v, sems.at[0]),
        pltpu.make_async_copy(a1, a1_v, sems.at[1]),
        pltpu.make_async_copy(y0.at[:, at], right.at[:tokens], sems.at[2]),
        pltpu.make_async_copy(y1.at[:, at], right.at[tokens:], sems.at[3]),
    ]
    for copy in copies:
        copy.start()
    copies[0].wait()
    copies[1].wait()
    wide = 512
    sent = []
    for step, out in enumerate(outs):
        for i in range(per):
            first, second = ORDER[per * step + i]
            to_x = lax.rem(x + jnp.where(c == 0, first, second), jnp.int32(side))
            to_y = lax.rem(y + jnp.where(c == 0, second, first), jnp.int32(side))
            column = pl.ds(pl.multiple_of((to_x * side + to_y) * rows, rows), rows)
            for token, a in enumerate((a0_v, a1_v)):
                block = a[:, column].T
                one, two = block[: rows // 2], block[rows // 2 :]
                there = slice(token * tokens, (token + 1) * tokens)
                left[step, i * rows : i * rows + rows // 2, there] = jnp.where(c == 0, one, two)
                left[step, i * rows + rows // 2 : (i + 1) * rows, there] = jnp.where(c == 0, two, one)
        if step == 0:
            copies[2].wait()
            copies[3].wait()
        for start in range(0, cols, wide):
            there = slice(start, start + wide)
            total = jnp.dot(left[step], right[:, there], preferred_element_type=f32)
            full[step, :, :, there] = total.astype(bf16).reshape(per, rows, wide)
        sent.append(pltpu.make_async_copy(full.at[step], out, out_sems.at[step]))
        sent[-1].start()
    for copy in sent:
        copy.wait()


def product(meta, a0, a1, y0, y1, side):
    tokens, dim = a0.shape
    cols = y1.shape[1] // 2
    rows = dim // (side * side)
    steps = side * side // 2
    return pl.pallas_call(
        functools.partial(product_body, side),
        out_shape=[shape((2, rows, cols), bf16)] * steps,
        in_specs=[SMEM] + [HBM] * 4,
        out_specs=[HBM] * steps,
        scratch_shapes=[
            pltpu.VMEM((tokens, dim), bf16),
            pltpu.VMEM((tokens, dim), bf16),
            pltpu.VMEM((steps, 2 * rows, 2 * tokens), bf16),
            pltpu.VMEM((2 * tokens, cols), bf16),
            pltpu.VMEM((steps, 2, rows, cols), bf16),
            pltpu.SemaphoreType.DMA((4,)),
            pltpu.SemaphoreType.DMA((steps,)),
        ],
        name="product",
        compiler_params=pltpu.CompilerParams(vmem_limit_bytes=62 * 2**20),
        cost_estimate=CHEAP,
    )(meta, a0, a1, y0, y1)


def after(a, *others):
    return lax.optimization_barrier((a,) + others)[0]


def exchange(a, axes):
    return lax.all_to_all(a, axes, 0, 0, tiled=True)


def role(a, phase, step, side):
    def at(x, y, c):
        return (x % side * side + y % side) * 2 + c

    pairs = []
    for x in range(side):
        for y in range(side):
            for c in range(2):
                if (c == 0) == (phase == 1):
                    pairs.append((at(x, y, c), at(x + step, y, c)))
                else:
                    pairs.append((at(x, y, c), at(x, y + step, c)))
    return lax.ppermute(a, SHARD, pairs)


def add(*arrays):
    return sum(a.astype(f32) for a in arrays).astype(bf16)


def on_device(acts, cot, error_prev, q_prev):
    x, y, c = (lax.axis_index(name).astype(jnp.int32) for name in SHARD)
    n_rep = lax.axis_size("z")
    side = lax.axis_size("x")
    n_shard = side * side * 2
    swap = [(0, 1), (1, 0)]
    err = error_prev[0]
    own, ffw = err.shape
    rank = q_prev.shape[1]
    dim = acts.shape[1]

    meta = ((x * side + y) * 2 + c)[None]

    acts_other = lax.ppermute(acts, "c", swap)
    cot_other = lax.ppermute(cot, "c", swap)

    parts = left(meta, q_prev.T, cot, acts, err, n_shard)
    g2a, g2b, g1b, g3a, g1a, g3b, g0a, g0b = product(
        after(meta, parts), acts, acts_other, cot, cot_other, side
    )
    parts = after(exchange(parts, SHARD), g0b)
    from2a = role(g2a, 1, 1, side)
    from2b = role(g2b, 1, -1, side)
    from1b = role(g1b, 1, 1, side)
    from3a = role(g3a, 1, -1, side)
    parts = total(parts, n_rep, f32, "left_shard")
    from2a, from2b = after(from2a, parts), after(from2b, parts)
    parts = after(exchange(parts, "z"), from2a, from2b)
    parts = total(parts, n_shard, f32, "left_rep")
    g1a = add(g1a, after(from2a, parts))
    g3b = add(g3b, after(from2b, parts))
    from1a = role(g1a, 1, 1, side)
    from3b = role(g3b, 1, -1, side)
    parts = after(exchange(parts, SHARD), g1a, g3b)

    high, wide = 16, rank * ffw // n_shard // 16
    blocks, own_hat = call(
        right_body, [shape((n_shard, high, wide), bf16), shape((rank, own), f32)],
        [(meta, SMEM), (parts, VMEM), (acts, HBM), (cot, HBM), (err, HBM)],
        "right",
        [pltpu.VMEM((rank, dim), f32)]
        + [pltpu.VMEM(a.shape, a.dtype) for a in (acts, cot, err)]
        + [pltpu.SemaphoreType.DMA((3,))],
        limit=56,
    )
    from1a, from3a, from1b, from3b = (after(a, blocks) for a in (from1a, from3a, from1b, from3b))
    ha = add(g0a, from1a, from3a)
    hb = add(g0b, from1b, from3b)
    near, far, back = role(ha[1], 2, 1, side), role(hb[0], 2, 2, side), role(hb[1], 2, -1, side)
    blocks = after(exchange(blocks, SHARD), ha, hb)
    blocks = total(blocks, n_rep, bf16, "right_shard", cost=CHEAP)
    near, far, back = (after(a, blocks) for a in (near, far, back))
    blocks = after(exchange(blocks, "z"), near, far, back)
    blocks = total(blocks, n_shard, bf16, "right_rep", 1.0 / n_rep)
    near, far, back = (after(a, blocks) for a in (near, far, back))
    theirs = lax.ppermute(add(ha[0, own:], near[own:], far[own:], back[own:]), "c", swap)
    mine = add(ha[0, :own], near[:own], far[:own], back[:own])
    blocks = exchange(blocks, SHARD)

    update, error_next, q_t = call(
        last_body, [shape((own, ffw), bf16), shape((own, ffw), f32), shape((rank, ffw), f32)],
        [(meta, SMEM), (blocks, VMEM), (own_hat, VMEM), (mine, VMEM), (theirs, VMEM), (err, VMEM)],
        "last", limit=8,
    )
    return update, error_next[None], q_t.T


def solution(mesh):
    reps, shards = mesh.devices.shape
    side = int((shards // 2) ** 0.5)
    grid = Mesh(mesh.devices.reshape(reps, side, side, 2), ("z",) + SHARD)
    every = ("z",) + SHARD
    return jax.shard_map(
        on_device,
        mesh=grid,
        in_specs=(P(every, None), P(every, None), P("z", SHARD, None), P()),
        out_specs=(P(SHARD, None), P("z", SHARD, None), P()),
        check_vma=False,
    )
```

profile of v0, /device:TPU:1, one launch (start us, length us, event | category | flops | bytes accessed | tf_op | source)
XLA Modules:
  0.0 140.7 jit_solution(12928664998844027663)
XLA Ops:
  0.6 3.3 %collective-permute-start.1 = (bf16[512,5120]{1,0:T(8,128)(2,1)}, bf16[512,5120]{1,0:T(8,128)(2,1)}, u32[]{:S(2)}, u32[]{:S(2)}) collective-permute-start(bf16[512,5120]{1,0:T(8,128)(2,1)} %cot_hbm.3), channel_id=1, source_target_pairs={{0,1},{1,0},{2,3},{3,2},{4,5},{5,4},{6,7},{7,6},{8,9},{9,8},{10,11... | collective-permute-start | bytes 15728648 | tf_op jit(solution)/shard_map/ppermute | solution.py:344
  4.0 0.1 collective-permute-start
  4.1 7.1 %left.1 = f32[32,8,512]{2,1,0:T(8,128)} custom-call(s32[1]{0:T(128)} %bitcast.meta, f32[64,5120]{1,0:T(8,128)} %bitcast.24, bf16[512,5120]{1,0:T(8,128)(2,1)} %cot_hbm.3, bf16[512,2048]{1,0:T(8,128)(2,1)} %acts_hbm.3, f32[64,5120]{1,0:T(8,128)} %bitcast.21), custom_call_target="tpu_custom_call" | custom-call | flops 49999998976 | bytes 1 | tf_op jit(solution)/shard_map/left/pallas_call | solution.py:42
  11.1 5.8 %all-to-all-start = ((f32[32,8,512]{2,1,0:T(8,128)}), f32[32,8,512]{2,1,0:T(8,128)S(1)}, u32[]{:S(2)}, u32[]{:S(2)}) async-start(f32[32,8,512]{2,1,0:T(8,128)} %left.1), calls=%async_computation | async-start | bytes 1048576 | tf_op jit(solution)/shard_map/all_to_all | solution.py:308
  16.9 0.0 collective-permute-done.a1
  16.9 0.0 collective-permute-done.1.y1
  16.9 16.1 %product.1 = (bf16[2,128,2560]{2,1,0:T(8,128)(2,1)}, bf16[2,128,2560]{2,1,0:T(8,128)(2,1)}, bf16[2,128,2560]{2,1,0:T(8,128)(2,1)}, bf16[2,128,2560]{2,1,0:T(8,12...) custom-call(s32[1]{0:T(128)} %bitcast.meta, ...), custom_call_target="tpu_custom_call" | custom-call | flops 1 | bytes 1 | tf_op jit(solution)/shard_map/product/pallas_call | solution.py:283
  33.0 0.0 all-to-all-done.part
  33.0 1.5 %collective-permute-start.2 = (bf16[2,128,2560]{2,1,0:T(8,128)(2,1)}, bf16[2,128,2560]{2,1,0:T(8,128)(2,1)}, u32[]{:S(2)}, u32[]{:S(2)}) collective-permute-start(bf16[2,128,2560]{2,1,0:T(8,128)(2,1)} %get-tuple-element.39), channel_id=1, source_target_pairs={{0,8},{1,3},{2,10},{3,5},{4,12},{5,7},{6,14},{7,1},{8,16},{9,11},{... | collective-permute-start | bytes 3932168 | tf_op jit(solution)/shard_map/ppermute | solution.py:323
  34.5 1.3 collective-permute-start.3
  35.8 0.7 left_shard.1
  36.5 8.2 %all-to-all-start.1 = ((f32[8,8,512]{2,1,0:T(8,128)}), f32[8,8,512]{2,1,0:T(8,128)S(1)}, u32[]{:S(2)}, u32[]{:S(2)}) async-start(f32[8,8,512]{2,1,0:T(8,128)} %left_shard.1), calls=%async_computation.1 | async-start | bytes 262144 | tf_op jit(solution)/shard_map/all_to_all | solution.py:308
  44.7 1.4 collective-permute-start.5
  46.1 0.1 collective-permute-start.6
  46.1 5.2 %collective-permute-done.2 = bf16[2,128,2560]{2,1,0:T(8,128)(2,1)} collective-permute-done((bf16[2,128,2560]{2,1,0:T(8,128)(2,1)}, bf16[2,128,2560]{2,1,0:T(8,128)(2,1)}, u32[]{:S(2)}, u32[]{:S(2)}) %collective-permute-start.2) | collective-permute-done | bytes 1310752 | tf_op jit(solution)/shard_map/ppermute | solution.py:323
  51.4 0.2 collective-permute-done.3
  51.5 1.1 copy-done.7
  52.6 0.0 all-to-all-done.1.part
  52.6 0.9 left_rep.1
  53.5 8.2 %all-to-all-start.2 = ((f32[32,8,512]{2,1,0:T(8,128)}), f32[32,8,512]{2,1,0:T(8,128)S(1)}, u32[]{:S(2)}, u32[]{:S(2)}) async-start(f32[32,8,512]{2,1,0:T(8,128)} %left_rep.1), calls=%async_computation.2 | async-start | bytes 1048576 | tf_op jit(solution)/shard_map/all_to_all | solution.py:308
  61.7 0.0 copy-done.6
  61.7 0.0 copy-start.5
  61.7 0.0 copy-start.8
  61.7 2.8 %add_convert_fusion.3 = bf16[2,128,2560]{2,1,0:T(8,128)(2,1)} fusion(bf16[2,128,2560]{2,1,0:T(8,128)(2,1)} %collective-permute-done.2, bf16[2,128,2560]{2,1,0:T(8,128)(2,1)S(1)} %copy-done.6), kind=kLoop, calls=%fused_computation.3 | loop fusion | flops 2621440 | bytes 3932160 | tf_op jit(solution)/shard_map/convert_element_type | solution.py:327
  64.6 1.4 collective-permute-start.4
  66.0 0.0 copy-done.5
  66.0 0.0 copy-done.8
  66.0 1.4 add_convert_fusion.2
  67.3 1.3 collective-permute-start.7
  68.6 6.1 %all-to-all-done.2.parts = f32[32,8,512]{2,1,0:T(8,128)S(1)} async-done(((f32[32,8,512]{2,1,0:T(8,128)}), f32[32,8,512]{2,1,0:T(8,128)S(1)}, u32[]{:S(2)}, u32[]{:S(2)}) %all-to-all-start.2) | async-done | bytes 524320 | tf_op jit(solution)/shard_map/all_to_all | solution.py:308
  74.7 0.8 copy-done.9
  75.5 7.8 %right.1 = (bf16[32,16,640]{2,1,0:T(8,128)(2,1)}, f32[64,64]{1,0:T(8,128)}) custom-call(s32[1]{0:T(128)} %bitcast.meta, f32[32,8,512]{2,1,0:T(8,128)} %copy-done.9, bf16[512,2048]{1,0:T(8,128)(2,1)} %acts_hbm.3, bf16[512,5120]{1,0:T(8,128)(2,1)} %cot_hbm.3, f32[64,5120]{1,0:T(8,128)} %bitcast.22), custom_call_target="tpu_custom_call" | custom-call | flops 49999998976 | bytes 1 | tf_op jit(solution)/shard_map/right/pallas_call | solution.py:42
  83.4 0.0 copy-start.4
  83.4 4.9 %all-to-all-start.3 = ((bf16[32,16,640]{2,1,0:T(8,128)(2,1)}), bf16[32,16,640]{2,1,0:T(8,128)(2,1)S(1)}, u32[]{:S(2)}, u32[]{:S(2)}) async-start(bf16[32,16,640]{2,1,0:T(8,128)(2,1)} %get-tuple-element.49), calls=%async_computation.3 | async-start | bytes 1310720 | tf_op jit(solution)/shard_map/all_to_all | solution.py:308
  88.2 0.0 collective-permute-done.5
  88.2 0.0 collective-permute-done.6
  88.3 0.0 collective-permute-done.4
  88.3 0.0 collective-permute-done.7
  88.3 0.0 copy-done.4
  88.3 2.2 %add_convert_fusion.1 = bf16[2,128,2560]{2,1,0:T(8,128)(2,1)S(1)} fusion(bf16[2,128,2560]{2,1,0:T(8,128)(2,1)} %collective-permute-done.5, bf16[2,128,2560]{2,1,0:T(8,128)(2,1)} %collective-permute-done.4, bf16[2,128,2560]{2,1,0:T(8,128)(2,1)S(1)} %copy-done.4), kind=kLoop, calls=%fused_computation.1 | loop fusion | flops 3932160 | bytes 5242880 | tf_op jit(solution)/shard_map/convert_element_type | solution.py:327
  90.5 0.0 copy-start.2
  90.5 0.0 copy-start.3
  90.5 1.0 copy-done.2
  91.5 1.4 collective-permute-start.8
  92.9 1.8 %add_convert_fusion = bf16[2,128,2560]{2,1,0:T(8,128)(2,1)S(1)} fusion(bf16[2,128,2560]{2,1,0:T(8,128)(2,1)} %collective-permute-done.7, bf16[2,128,2560]{2,1,0:T(8,128)(2,1)S(1)} %collective-permute-done.6, bf16[2,128,2560]{2,1,0:T(8,128)(2,1)S(1)} %copy-done.3), kind=kLoop, calls=%fused_computation | loop fusion | flops 3932160 | bytes 5242880 | tf_op jit(solution)/shard_map/convert_element_type | solution.py:327
  94.7 0.1 slice_bitcast_fusion
  94.8 2.1 %collective-permute-start.10 = (bf16[128,2560]{1,0:T(8,128)(2,1)S(1)}, bf16[128,2560]{1,0:T(8,128)(2,1)}, u32[]{:S(2)}, u32[]{:S(2)}) collective-permute-start(bf16[128,2560]{1,0:T(8,128)(2,1)S(1)} %get-tuple-element.71), channel_id=1, source_target_pairs={{0,6},{1,25},{2,0},{3,27},{4,2},{5,29},{6,4},{7,31},{8,14},{9,1},{... | collective-permute-start | bytes 1966088 | tf_op jit(solution)/shard_map/ppermute | solution.py:323
  96.9 1.0 collective-permute-start.9
  97.9 3.4 %all-to-all-done.3.part = bf16[32,16,640]{2,1,0:T(8,128)(2,1)S(1)} async-done(((bf16[32,16,640]{2,1,0:T(8,128)(2,1)}), bf16[32,16,640]{2,1,0:T(8,128)(2,1)S(1)}, u32[]{:S(2)}, u32[]{:S(2)}) %all-to-all-start.3) | async-done | bytes 655392 | tf_op jit(solution)/shard_map/all_to_all | solution.py:308
  101.3 0.8 right_shard.1
  102.0 8.2 %all-to-all-start.4 = ((bf16[8,16,640]{2,1,0:T(8,128)(2,1)}), bf16[8,16,640]{2,1,0:T(8,128)(2,1)S(1)}, u32[]{:S(2)}, u32[]{:S(2)}) async-start(bf16[8,16,640]{2,1,0:T(8,128)(2,1)} %right_shard.1), calls=%async_computation.4 | async-start | bytes 327680 | tf_op jit(solution)/shard_map/all_to_all | solution.py:308
  110.2 0.0 collective-permute-done.8
  110.2 1.2 collective-permute-done.10
  111.4 2.2 %collective-permute-done.9 = bf16[128,2560]{1,0:T(8,128)(2,1)} collective-permute-done((bf16[128,2560]{1,0:T(8,128)(2,1)S(1)}, bf16[128,2560]{1,0:T(8,128)(2,1)}, u32[]{:S(2)}, u32[]{:S(2)}) %collective-permute-start.9) | collective-permute-done | bytes 655392 | tf_op jit(solution)/shard_map/ppermute | solution.py:323
  113.6 6.8 %all-to-all-done.4.part = bf16[8,16,640]{2,1,0:T(8,128)(2,1)S(1)} async-done(((bf16[8,16,640]{2,1,0:T(8,128)(2,1)}), bf16[8,16,640]{2,1,0:T(8,128)(2,1)S(1)}, u32[]{:S(2)}, u32[]{:S(2)}) %all-to-all-start.4) | async-done | bytes 163872 | tf_op jit(solution)/shard_map/all_to_all | solution.py:308
  120.5 0.9 right_rep.1
  121.4 4.0 %all-to-all-start.5 = ((bf16[32,16,640]{2,1,0:T(8,128)(2,1)}), bf16[32,16,640]{2,1,0:T(8,128)(2,1)S(1)}, u32[]{:S(2)}, u32[]{:S(2)}) async-start(bf16[32,16,640]{2,1,0:T(8,128)(2,1)} %right_rep.1), calls=%async_computation.5 | async-start | bytes 1310720 | tf_op jit(solution)/shard_map/all_to_all | solution.py:308
  125.4 0.0 copy-start
  125.4 1.9 %fusion.2 = (bf16[64,2560]{1,0:T(8,128)(2,1)S(1)}, bf16[64,2560]{1,0:T(8,128)(2,1)S(1)}) fusion(bf16[2,128,2560]{2,1,0:T(8,128)(2,1)} %copy-done.2, bf16[128,2560]{1,0:T(8,128)(2,1)} %collective-permute-done.10, bf16[128,2560]{1,0:T(8,128)(2,1)} %collective-permute-done.9, bf16[128,2560]{1,0:T(8,128)(2,1)S(1)} %collective-permute-done.8), kind=kLoop, calls=%fused_computation.10 | loop fusion | flops 2621440 | bytes 3276800 | tf_op jit(solution)/shard_map/convert_element_type | solution.py:327
  127.3 0.4 collective-permute-start.11
  127.8 1.3 collective-permute-done.11.theirs
  129.0 9.4 %all-to-all-done.5.parts = bf16[32,16,640]{2,1,0:T(8,128)(2,1)S(1)} async-done(((bf16[32,16,640]{2,1,0:T(8,128)(2,1)}), bf16[32,16,640]{2,1,0:T(8,128)(2,1)S(1)}, u32[]{:S(2)}, u32[]{:S(2)}) %all-to-all-start.5) | async-done | bytes 655392 | tf_op jit(solution)/shard_map/all_to_all | solution.py:308
  138.5 0.0 copy-done.1
  138.5 2.2 %last.1 = (bf16[64,5120]{1,0:T(8,128)(2,1)}, f32[64,5120]{1,0:T(8,128)}, f32[64,5120]{1,0:T(8,128)}) custom-call(s32[1]{0:T(128)} %bitcast.meta, bf16[32,16,640]{2,1,0:T(8,128)(2,1)S(1)} %all-to-all-done.5.parts, f32[64,64]{1,0:T(8,128)S(1)} %copy-done.1, bf16[64,2560]{1,0:T(8,128)(2,1)S(1)} %get-tuple-element.70.mine, ...), custom_call_target="tpu_custom_call" | custom-call | flops 49999998976 | bytes 1 | tf_op jit(solution)/shard_map/last/pallas_call | solution.py:42
  (7 shorter events, 0.1 us)
Async XLA Ops:
  0.6 16.3 %collective-permute-start.1 = (bf16[512,5120]{1,0:T(8,128)(2,1)}, bf16[512,5120]{1,0:T(8,128)(2,1)}, u32[]{:S(2)}, u32[]{:S(2)}) collective-permute-start(bf16[512,5120]{1,0:T(8,128)(2,1)} %cot_hbm.3), channel_id=1, source_target_pairs={{0,1},{1,0},{2,3},{3,2},{4,5},{5,4},{6,7},{7,6},{8,9},{9,8},{10,11... | collective-permute-start | bytes 15728648 | tf_op jit(solution)/shard_map/ppermute | solution.py:344
  4.0 12.9 %collective-permute-start = (bf16[512,2048]{1,0:T(8,128)(2,1)}, bf16[512,2048]{1,0:T(8,128)(2,1)}, u32[]{:S(2)}, u32[]{:S(2)}) collective-permute-start(bf16[512,2048]{1,0:T(8,128)(2,1)} %acts_hbm.3), channel_id=1, source_target_pairs={{0,1},{1,0},{2,3},{3,2},{4,5},{5,4},{6,7},{7,6},{8,9},{9,8},{10,11... | collective-permute-start | bytes 6291464 | tf_op jit(solution)/shard_map/ppermute | solution.py:343
  11.1 21.9 %all-to-all-start = ((f32[32,8,512]{2,1,0:T(8,128)}), f32[32,8,512]{2,1,0:T(8,128)S(1)}, u32[]{:S(2)}, u32[]{:S(2)}) async-start(f32[32,8,512]{2,1,0:T(8,128)} %left.1), calls=%async_computation | async-start | bytes 1048576 | tf_op jit(solution)/shard_map/all_to_all | solution.py:308
  33.0 18.4 %collective-permute-start.2 = (bf16[2,128,2560]{2,1,0:T(8,128)(2,1)}, bf16[2,128,2560]{2,1,0:T(8,128)(2,1)}, u32[]{:S(2)}, u32[]{:S(2)}) collective-permute-start(bf16[2,128,2560]{2,1,0:T(8,128)(2,1)} %get-tuple-element.39), channel_id=1, source_target_pairs={{0,8},{1,3},{2,10},{3,5},{4,12},{5,7},{6,14},{7,1},{8,16},{9,11},{... | collective-permute-start | bytes 3932168 | tf_op jit(solution)/shard_map/ppermute | solution.py:323
  34.5 17.1 %collective-permute-start.3 = (bf16[2,128,2560]{2,1,0:T(8,128)(2,1)}, bf16[2,128,2560]{2,1,0:T(8,128)(2,1)S(1)}, u32[]{:S(2)}, u32[]{:S(2)}) collective-permute-start(bf16[2,128,2560]{2,1,0:T(8,128)(2,1)} %get-tuple-element.41), channel_id=1, source_target_pairs={{0,24},{1,7},{2,26},{3,1},{4,28},{5,3},{6,30},{7,5},{8,0},{9,15},{... | collective-permute-start | bytes 3932168 | tf_op jit(solution)/shard_map/ppermute | solution.py:323
  36.5 16.1 %all-to-all-start.1 = ((f32[8,8,512]{2,1,0:T(8,128)}), f32[8,8,512]{2,1,0:T(8,128)S(1)}, u32[]{:S(2)}, u32[]{:S(2)}) async-start(f32[8,8,512]{2,1,0:T(8,128)} %left_shard.1), calls=%async_computation.1 | async-start | bytes 262144 | tf_op jit(solution)/shard_map/all_to_all | solution.py:308
  44.7 43.6 %collective-permute-start.5 = (bf16[2,128,2560]{2,1,0:T(8,128)(2,1)}, bf16[2,128,2560]{2,1,0:T(8,128)(2,1)}, u32[]{:S(2)}, u32[]{:S(2)}) collective-permute-start(bf16[2,128,2560]{2,1,0:T(8,128)(2,1)} %get-tuple-element.52), channel_id=1, source_target_pairs={{0,24},{1,7},{2,26},{3,1},{4,28},{5,3},{6,30},{7,5},{8,0},{9,15},{... | collective-permute-start | bytes 3932168 | tf_op jit(solution)/shard_map/ppermute | solution.py:323
  46.1 42.2 %collective-permute-start.6 = (bf16[2,128,2560]{2,1,0:T(8,128)(2,1)}, bf16[2,128,2560]{2,1,0:T(8,128)(2,1)S(1)}, u32[]{:S(2)}, u32[]{:S(2)}) collective-permute-start(bf16[2,128,2560]{2,1,0:T(8,128)(2,1)} %get-tuple-element.54), channel_id=1, source_target_pairs={{0,8},{1,3},{2,10},{3,5},{4,12},{5,7},{6,14},{7,1},{8,16},{9,11},{... | collective-permute-start | bytes 3932168 | tf_op jit(solution)/shard_map/ppermute | solution.py:323
  51.5 1.1 copy-start.7
  52.6 9.1 %copy-start.6 = (bf16[2,128,2560]{2,1,0:T(8,128)(2,1)S(1)}, bf16[2,128,2560]{2,1,0:T(8,128)(2,1)}, u32[]{:S(2)}) copy-start(bf16[2,128,2560]{2,1,0:T(8,128)(2,1)} %get-tuple-element.44) | copy-start | bytes 3932164
  53.5 21.2 %all-to-all-start.2 = ((f32[32,8,512]{2,1,0:T(8,128)}), f32[32,8,512]{2,1,0:T(8,128)S(1)}, u32[]{:S(2)}, u32[]{:S(2)}) async-start(f32[32,8,512]{2,1,0:T(8,128)} %left_rep.1), calls=%async_computation.2 | async-start | bytes 1048576 | tf_op jit(solution)/shard_map/all_to_all | solution.py:308
  61.7 4.2 %copy-start.5 = (bf16[2,128,2560]{2,1,0:T(8,128)(2,1)S(1)}, bf16[2,128,2560]{2,1,0:T(8,128)(2,1)}, u32[]{:S(2)}) copy-start(bf16[2,128,2560]{2,1,0:T(8,128)(2,1)} %get-tuple-element.46) | copy-start | bytes 3932164
  61.7 4.2 %copy-start.8 = (bf16[2,128,2560]{2,1,0:T(8,128)(2,1)S(1)}, bf16[2,128,2560]{2,1,0:T(8,128)(2,1)}, u32[]{:S(2)}) copy-start(bf16[2,128,2560]{2,1,0:T(8,128)(2,1)} %copy-done.7) | copy-start | bytes 3932164
  64.6 23.7 %collective-permute-start.4 = (bf16[2,128,2560]{2,1,0:T(8,128)(2,1)}, bf16[2,128,2560]{2,1,0:T(8,128)(2,1)}, u32[]{:S(2)}, u32[]{:S(2)}) collective-permute-start(bf16[2,128,2560]{2,1,0:T(8,128)(2,1)} %add_convert_fusion.3), channel_id=1, source_target_pairs={{0,8},{1,3},{2,10},{3,5},{4,12},{5,7},{6,14},{7,1},{8,16},{9,11},{... | collective-permute-start | bytes 3932168 | tf_op jit(solution)/shard_map/ppermute | solution.py:323
  67.3 20.9 %collective-permute-start.7 = (bf16[2,128,2560]{2,1,0:T(8,128)(2,1)}, bf16[2,128,2560]{2,1,0:T(8,128)(2,1)}, u32[]{:S(2)}, u32[]{:S(2)}) collective-permute-start(bf16[2,128,2560]{2,1,0:T(8,128)(2,1)} %add_convert_fusion.2), channel_id=1, source_target_pairs={{0,24},{1,7},{2,26},{3,1},{4,28},{5,3},{6,30},{7,5},{8,0},{9,15},{... | collective-permute-start | bytes 3932168 | tf_op jit(solution)/shard_map/ppermute | solution.py:323
  74.7 0.8 copy-start.9
  83.4 4.9 %copy-start.4 = (bf16[2,128,2560]{2,1,0:T(8,128)(2,1)S(1)}, bf16[2,128,2560]{2,1,0:T(8,128)(2,1)}, u32[]{:S(2)}) copy-start(bf16[2,128,2560]{2,1,0:T(8,128)(2,1)} %get-tuple-element.50) | copy-start | bytes 3932164
  83.4 17.9 %all-to-all-start.3 = ((bf16[32,16,640]{2,1,0:T(8,128)(2,1)}), bf16[32,16,640]{2,1,0:T(8,128)(2,1)S(1)}, u32[]{:S(2)}, u32[]{:S(2)}) async-start(bf16[32,16,640]{2,1,0:T(8,128)(2,1)} %get-tuple-element.49), calls=%async_computation.3 | async-start | bytes 1310720 | tf_op jit(solution)/shard_map/all_to_all | solution.py:308
  90.5 1.1 copy-start.2
  90.5 2.4 %copy-start.3 = (bf16[2,128,2560]{2,1,0:T(8,128)(2,1)S(1)}, bf16[2,128,2560]{2,1,0:T(8,128)(2,1)}, u32[]{:S(2)}) copy-start(bf16[2,128,2560]{2,1,0:T(8,128)(2,1)} %get-tuple-element.37) | copy-start | bytes 3932164
  91.5 18.7 %collective-permute-start.8 = (bf16[128,2560]{1,0:T(8,128)(2,1)S(1)}, bf16[128,2560]{1,0:T(8,128)(2,1)S(1)}, u32[]{:S(2)}, u32[]{:S(2)}) collective-permute-start(bf16[128,2560]{1,0:T(8,128)(2,1)S(1)} %slice_bitcast_fusion.2), channel_id=1, source_target_pairs={{0,2},{1,9},{2,4},{3,11},{4,6},{5,13},{6,0},{7,15},{8,10},{9,17},{... | collective-permute-start | bytes 1966088 | tf_op jit(solution)/shard_map/ppermute | solution.py:323
  94.8 16.6 %collective-permute-start.10 = (bf16[128,2560]{1,0:T(8,128)(2,1)S(1)}, bf16[128,2560]{1,0:T(8,128)(2,1)}, u32[]{:S(2)}, u32[]{:S(2)}) collective-permute-start(bf16[128,2560]{1,0:T(8,128)(2,1)S(1)} %get-tuple-element.71), channel_id=1, source_target_pairs={{0,6},{1,25},{2,0},{3,27},{4,2},{5,29},{6,4},{7,31},{8,14},{9,1},{... | collective-permute-start | bytes 1966088 | tf_op jit(solution)/shard_map/ppermute | solution.py:323
  96.9 16.8 %collective-permute-start.9 = (bf16[128,2560]{1,0:T(8,128)(2,1)S(1)}, bf16[128,2560]{1,0:T(8,128)(2,1)}, u32[]{:S(2)}, u32[]{:S(2)}) collective-permute-start(bf16[128,2560]{1,0:T(8,128)(2,1)S(1)} %get-tuple-element.72), channel_id=1, source_target_pairs={{0,4},{1,17},{2,6},{3,19},{4,0},{5,21},{6,2},{7,23},{8,12},{9,25},... | collective-permute-start | bytes 1966088 | tf_op jit(solution)/shard_map/ppermute | solution.py:323
  102.0 18.4 %all-to-all-start.4 = ((bf16[8,16,640]{2,1,0:T(8,128)(2,1)}), bf16[8,16,640]{2,1,0:T(8,128)(2,1)S(1)}, u32[]{:S(2)}, u32[]{:S(2)}) async-start(bf16[8,16,640]{2,1,0:T(8,128)(2,1)} %right_shard.1), calls=%async_computation.4 | async-start | bytes 327680 | tf_op jit(solution)/shard_map/all_to_all | solution.py:308
  121.4 17.1 %all-to-all-start.5 = ((bf16[32,16,640]{2,1,0:T(8,128)(2,1)}), bf16[32,16,640]{2,1,0:T(8,128)(2,1)S(1)}, u32[]{:S(2)}, u32[]{:S(2)}) async-start(bf16[32,16,640]{2,1,0:T(8,128)(2,1)} %right_rep.1), calls=%async_computation.5 | async-start | bytes 1310720 | tf_op jit(solution)/shard_map/all_to_all | solution.py:308
  125.4 13.1 %copy-start = (f32[1,64,5120]{2,1,0:T(8,128)S(1)}, f32[1,64,5120]{2,1,0:T(8,128)}, u32[]{:S(2)}) copy-start(f32[1,64,5120]{2,1,0:T(8,128)} %param.6) | copy-start | bytes 3932164
  125.4 13.0 %copy-start.1 = (f32[64,64]{1,0:T(8,128)S(1)}, f32[64,64]{1,0:T(8,128)}, u32[]{:S(2)}) copy-start(f32[64,64]{1,0:T(8,128)} %get-tuple-element.62.own_t) | copy-start | bytes 49156
  127.3 1.7 %collective-permute-start.11 = (bf16[64,2560]{1,0:T(8,128)(2,1)S(1)}, bf16[64,2560]{1,0:T(8,128)(2,1)S(1)}, u32[]{:S(2)}, u32[]{:S(2)}) collective-permute-start(bf16[64,2560]{1,0:T(8,128)(2,1)S(1)} %get-tuple-element.69), channel_id=1, source_target_pairs={{0,1},{1,0},{2,3},{3,2},{4,5},{5,4},{6,7},{7,6},{8,9},{9,8},{10,11... | collective-permute-start | bytes 983048 | tf_op jit(solution)/shard_map/ppermute | solution.py:385
where the time goes:
time: 141 us
  starting transfers between devices  54.4 us (39%)
  Pallas kernels  36.4 us (26%)
  waiting for transfers between devices  35.9 us (25%)
  other arithmetic  10.1 us (7%)
  local copies, waits for them, and re-layouts  3.02 us (2%)
    all_to_all x6, starting transfers between devices, exchange(): return lax.all_to_all(a, axes, 0, 0, tiled=True)  39.2 us
    all_to_all x6, waiting for transfers between devices, exchange(): return lax.all_to_all(a, axes, 0, 0, tiled=True)  25.8 us
    pallas_call x7, Pallas kernels, call(): pl.pallas_call(body, out_shape=outs, in_specs=[spec for _, spec in ins],...  20.3 us
    pallas_call x1, Pallas kernels, product(): pl.pallas_call(functools.partial(product_body, side), out_shape=[shape((2...  16.1 us
    ppermute x9, starting transfers between devices, role(): return lax.ppermute(a, SHARD, pairs)  11.4 us
    convert_element_type x5, other arithmetic, add(): return sum((a.astype(f32) for a in arrays)).astype(bf16)  10.1 us
    ppermute x9, waiting for transfers between devices, role(): return lax.ppermute(a, SHARD, pairs)  8.83 us
    ppermute x1, starting transfers between devices, on_device(): cot_other = lax.ppermute(cot, 'c', swap)  3.33 us
  transfers between devices with their start and end apart: 18, of which 9 were waited for; matrix products, arithmetic and copies ran while one was open for 7% of the time, Pallas kernels for 24%

commit v1 on v0

--- a/solution.py
+++ b/solution.py
@@ -38,12 +38,12 @@
     return a[:size] + a[size:]
 
 
-def call(body, outs, ins, name, scratch=(), limit=8, cost=CHAIN):
+def call(body, outs, ins, name, scratch=(), limit=8, cost=CHAIN, place=VMEM):
     return pl.pallas_call(
         body,
         out_shape=outs,
         in_specs=[spec for _, spec in ins],
-        out_specs=[VMEM] * len(outs),
+        out_specs=[place] * len(outs),
         scratch_shapes=list(scratch),
         name=name,
         compiler_params=pltpu.CompilerParams(vmem_limit_bytes=limit * 2**20),
@@ -203,7 +203,8 @@
             out[g * across + l] = q[g * high : (g + 1) * high]
 
 
-def last_body(meta, parts, own_t, mine, theirs, err, update, error_next, q_out):
+def last_body(meta, parts, own_t, mine, theirs, err, update_hbm, error_hbm, q_hbm, update, error_next, q_out, sems):
+    sent = []
     _, high, wide = parts.shape
     rank = own_t.shape[0]
     across = err.shape[1] // wide
@@ -220,6 +221,11 @@
         there = slice(at, at + wide)
         grad = jnp.where(c == side, mine[:, there].astype(f32), theirs[:, there].astype(f32))
         error_next[:, cols] = grad + err[:, cols] - full
+        for a, to in ((update, update_hbm), (error_next, error_hbm), (q_out, q_hbm)):
+            sent.append(pltpu.make_async_copy(a.at[:, cols], to.at[:, cols], sems.at[len(sent)]))
+            sent[-1].start()
+    for copy in sent:
+        copy.wait()
 
 
 ORDER = [(2, 0), (2, 1), (2, 2), (2, 3), (1, 2), (1, 3), (3, 0), (3, 1)]
@@ -233,38 +239,50 @@
 
 
 def product_body(side, meta, a0, a1, y0, y1, *refs):
-    outs, (a0_v, a1_v, left, right, full, sems, out_sems) = refs[:-7], refs[-7:]
+    outs, (soon, a0_v, a1_v, left, right, full, sems, soon_sems, out_sems) = refs[:-9], refs[-9:]
     _, per, rows, cols = full.shape
     tokens = a0.shape[0]
     c, x, y = place_of(meta[0], side)
+
+    def column(n):
+        first, second = ORDER[n]
+        to_x = lax.rem(x + jnp.where(c == 0, first, second), jnp.int32(side))
+        to_y = lax.rem(y + jnp.where(c == 0, second, first), jnp.int32(side))
+        return pl.ds(pl.multiple_of((to_x * side + to_y) * rows, rows), rows)
+
     at = pl.ds(pl.multiple_of(c * cols, 128), cols)
-    copies = [
-        pltpu.make_async_copy(a0, a0_v, sems.at[0]),
-        pltpu.make_async_copy(a1, a1_v, sems.at[1]),
-        pltpu.make_async_copy(y0.at[:, at], right.at[:tokens], sems.at[2]),
-        pltpu.make_async_copy(y1.at[:, at], right.at[tokens:], sems.at[3]),
+    early = [
+        pltpu.make_async_copy(a.at[:, column(i)], soon.at[2 * i + token], soon_sems.at[2 * i + token])
+        for i in range(per)
+        for token, a in enumerate((a0, a1))
     ]
-    for copy in copies:
+    feed = [
+        pltpu.make_async_copy(y0.at[:, at], right.at[:tokens], sems.at[0]),
+        pltpu.make_async_copy(y1.at[:, at], right.at[tokens:], sems.at[1]),
+    ]
+    rest = [
+        pltpu.make_async_copy(a0, a0_v, sems.at[2]),
+        pltpu.make_async_copy(a1, a1_v, sems.at[3]),
+    ]
+    for copy in early + feed:
         copy.start()
-    copies[0].wait()
-    copies[1].wait()
     wide = 512
     sent = []
     for step, out in enumerate(outs):
+        for copy in early if step == 0 else rest if step == 1 else []:
+            copy.wait()
         for i in range(per):
-            first, second = ORDER[per * step + i]
-            to_x = lax.rem(x + jnp.where(c == 0, first, second), jnp.int32(side))
-            to_y = lax.rem(y + jnp.where(c == 0, second, first), jnp.int32(side))
-            column = pl.ds(pl.multiple_of((to_x * side + to_y) * rows, rows), rows)
             for token, a in enumerate((a0_v, a1_v)):
-                block = a[:, column].T
+                block = (soon[2 * i + token] if step == 0 else a[:, column(per * step + i)]).T
                 one, two = block[: rows // 2], block[rows // 2 :]
                 there = slice(token * tokens, (token + 1) * tokens)
                 left[step, i * rows : i * rows + rows // 2, there] = jnp.where(c == 0, one, two)
                 left[step, i * rows + rows // 2 : (i + 1) * rows, there] = jnp.where(c == 0, two, one)
         if step == 0:
-            copies[2].wait()
-            copies[3].wait()
+            for copy in feed:
+                copy.wait()
+            for copy in rest:
+                copy.start()
         for start in range(0, cols, wide):
             there = slice(start, start + wide)
             total = jnp.dot(left[step], right[:, there], preferred_element_type=f32)
@@ -286,11 +304,13 @@
         in_specs=[SMEM] + [HBM] * 4,
         out_specs=[HBM] * steps,
         scratch_shapes=[
+            pltpu.VMEM((4, tokens, rows), bf16),
             pltpu.VMEM((tokens, dim), bf16),
             pltpu.VMEM((tokens, dim), bf16),
             pltpu.VMEM((steps, 2 * rows, 2 * tokens), bf16),
             pltpu.VMEM((2 * tokens, cols), bf16),
             pltpu.VMEM((steps, 2, rows, cols), bf16),
+            pltpu.SemaphoreType.DMA((4,)),
             pltpu.SemaphoreType.DMA((4,)),
             pltpu.SemaphoreType.DMA((steps,)),
         ],
@@ -386,10 +406,14 @@
     mine = add(ha[0, :own], near[:own], far[:own], back[:own])
     blocks = exchange(blocks, SHARD)
 
+    outs = [shape((own, ffw), bf16), shape((own, ffw), f32), shape((rank, ffw), f32)]
     update, error_next, q_t = call(
-        last_body, [shape((own, ffw), bf16), shape((own, ffw), f32), shape((rank, ffw), f32)],
+        last_body, outs,
         [(meta, SMEM), (blocks, VMEM), (own_hat, VMEM), (mine, VMEM), (theirs, VMEM), (err, VMEM)],
-        "last", limit=8,
+        "last",
+        [pltpu.VMEM(out.shape, out.dtype) for out in outs]
+        + [pltpu.SemaphoreType.DMA((3 * n_shard * 16 // rank,))],
+        limit=16, place=HBM,
     )
     return update, error_next[None], q_t.T
 

time: 141 us -> 142 us (level)
  no operation moved by 1% of the time
where the time goes in v1:
time: 142 us; the launch traced here: 141 us
  starting transfers between devices  54.4 us (38%)
  Pallas kernels  36.4 us (26%)
  waiting for transfers between devices  35.9 us (25%)
  other arithmetic  10.1 us (7%)
  local copies, waits for them, and re-layouts  3.02 us (2%)
    all_to_all x6, starting transfers between devices, exchange(): return lax.all_to_all(a, axes, 0, 0, tiled=True)  39.2 us
    all_to_all x6, waiting for transfers between devices, exchange(): return lax.all_to_all(a, axes, 0, 0, tiled=True)  25.8 us
    pallas_call x7, Pallas kernels, call(): pl.pallas_call(body, out_shape=outs, in_specs=[spec for _, spec in ins],...  20.3 us
    pallas_call x1, Pallas kernels, product(): pl.pallas_call(functools.partial(product_body, side), out_shape=[shape((2...  16.1 us
    ppermute x9, starting transfers between devices, role(): return lax.ppermute(a, SHARD, pairs)  11.3 us
    convert_element_type x5, other arithmetic, add(): return sum((a.astype(f32) for a in arrays)).astype(bf16)  10.1 us
    ppermute x9, waiting for transfers between devices, role(): return lax.ppermute(a, SHARD, pairs)  8.81 us
    ppermute x1, starting transfers between devices, on_device(): cot_other = lax.ppermute(cot, 'c', swap)  3.33 us
  transfers between devices with their start and end apart: 18, of which 9 were waited for; matrix products, arithmetic and copies ran while one was open for 7% of the time, Pallas kernels for 24%

profile of v1, /device:TPU:1, one launch (start us, length us, event | category | flops | bytes accessed | tf_op | source)
XLA Modules:
  0.0 140.9 jit_solution(15531039891825151210)
XLA Ops:
  0.6 3.3 %collective-permute-start.1 = (bf16[512,5120]{1,0:T(8,128)(2,1)}, bf16[512,5120]{1,0:T(8,128)(2,1)}, u32[]{:S(2)}, u32[]{:S(2)}) collective-permute-start(bf16[512,5120]{1,0:T(8,128)(2,1)} %cot_hbm.3), channel_id=1, source_target_pairs={{0,1},{1,0},{2,3},{3,2},{4,5},{5,4},{6,7},{7,6},{8,9},{9,8},{10,11... | collective-permute-start | bytes 15728648 | tf_op jit(solution)/shard_map/ppermute | solution.py:364
  4.0 0.1 collective-permute-start
  4.1 7.1 %left.1 = f32[32,8,512]{2,1,0:T(8,128)} custom-call(s32[1]{0:T(128)} %bitcast.meta, f32[64,5120]{1,0:T(8,128)} %bitcast.24, bf16[512,5120]{1,0:T(8,128)(2,1)} %cot_hbm.3, bf16[512,2048]{1,0:T(8,128)(2,1)} %acts_hbm.3, f32[64,5120]{1,0:T(8,128)} %bitcast.21), custom_call_target="tpu_custom_call" | custom-call | flops 49999998976 | bytes 1 | tf_op jit(solution)/shard_map/left/pallas_call | solution.py:42
  11.1 5.8 %all-to-all-start = ((f32[32,8,512]{2,1,0:T(8,128)}), f32[32,8,512]{2,1,0:T(8,128)S(1)}, u32[]{:S(2)}, u32[]{:S(2)}) async-start(f32[32,8,512]{2,1,0:T(8,128)} %left.1), calls=%async_computation | async-start | bytes 1048576 | tf_op jit(solution)/shard_map/all_to_all | solution.py:328
  16.9 0.0 collective-permute-done.a1
  16.9 0.0 collective-permute-done.1.y1
  16.9 16.1 %product.1 = (bf16[2,128,2560]{2,1,0:T(8,128)(2,1)}, bf16[2,128,2560]{2,1,0:T(8,128)(2,1)}, bf16[2,128,2560]{2,1,0:T(8,128)(2,1)}, bf16[2,128,2560]{2,1,0:T(8,12...) custom-call(s32[1]{0:T(128)} %bitcast.meta, ...), custom_call_target="tpu_custom_call" | custom-call | flops 1 | bytes 1 | tf_op jit(solution)/shard_map/product/pallas_call | solution.py:301
  33.0 0.0 all-to-all-done.part
  33.0 1.4 %collective-permute-start.2 = (bf16[2,128,2560]{2,1,0:T(8,128)(2,1)}, bf16[2,128,2560]{2,1,0:T(8,128)(2,1)}, u32[]{:S(2)}, u32[]{:S(2)}) collective-permute-start(bf16[2,128,2560]{2,1,0:T(8,128)(2,1)} %get-tuple-element.39), channel_id=1, source_target_pairs={{0,8},{1,3},{2,10},{3,5},{4,12},{5,7},{6,14},{7,1},{8,16},{9,11},{... | collective-permute-start | bytes 3932168 | tf_op jit(solution)/shard_map/ppermute | solution.py:343
  34.5 1.3 collective-permute-start.3
  35.8 0.7 left_shard.1
  36.5 8.2 %all-to-all-start.1 = ((f32[8,8,512]{2,1,0:T(8,128)}), f32[8,8,512]{2,1,0:T(8,128)S(1)}, u32[]{:S(2)}, u32[]{:S(2)}) async-start(f32[8,8,512]{2,1,0:T(8,128)} %left_shard.1), calls=%async_computation.1 | async-start | bytes 262144 | tf_op jit(solution)/shard_map/all_to_all | solution.py:328
  44.7 1.4 collective-permute-start.5
  46.1 0.1 collective-permute-start.6
  46.2 5.2 %collective-permute-done.2 = bf16[2,128,2560]{2,1,0:T(8,128)(2,1)} collective-permute-done((bf16[2,128,2560]{2,1,0:T(8,128)(2,1)}, bf16[2,128,2560]{2,1,0:T(8,128)(2,1)}, u32[]{:S(2)}, u32[]{:S(2)}) %collective-permute-start.2) | collective-permute-done | bytes 1310752 | tf_op jit(solution)/shard_map/ppermute | solution.py:343
  51.4 0.1 collective-permute-done.3
  51.6 1.1 copy-done.7
  52.6 0.0 all-to-all-done.1.part
  52.6 0.9 left_rep.1
  53.5 8.2 %all-to-all-start.2 = ((f32[32,8,512]{2,1,0:T(8,128)}), f32[32,8,512]{2,1,0:T(8,128)S(1)}, u32[]{:S(2)}, u32[]{:S(2)}) async-start(f32[32,8,512]{2,1,0:T(8,128)} %left_rep.1), calls=%async_computation.2 | async-start | bytes 1048576 | tf_op jit(solution)/shard_map/all_to_all | solution.py:328
  61.7 0.0 copy-done.6
  61.7 0.0 copy-start.5
  61.7 0.0 copy-start.8
  61.7 2.8 %add_convert_fusion.3 = bf16[2,128,2560]{2,1,0:T(8,128)(2,1)} fusion(bf16[2,128,2560]{2,1,0:T(8,128)(2,1)} %collective-permute-done.2, bf16[2,128,2560]{2,1,0:T(8,128)(2,1)S(1)} %copy-done.6), kind=kLoop, calls=%fused_computation.3 | loop fusion | flops 2621440 | bytes 3932160 | tf_op jit(solution)/shard_map/convert_element_type | solution.py:347
  64.6 1.4 collective-permute-start.4
  66.0 0.0 copy-done.5
  66.0 0.0 copy-done.8
  66.0 1.4 add_convert_fusion.2
  67.3 1.3 collective-permute-start.7
  68.6 6.1 %all-to-all-done.2.parts = f32[32,8,512]{2,1,0:T(8,128)S(1)} async-done(((f32[32,8,512]{2,1,0:T(8,128)}), f32[32,8,512]{2,1,0:T(8,128)S(1)}, u32[]{:S(2)}, u32[]{:S(2)}) %all-to-all-start.2) | async-done | bytes 524320 | tf_op jit(solution)/shard_map/all_to_all | solution.py:328
  74.7 0.8 copy-done.9
  75.6 7.8 %right.1 = (bf16[32,16,640]{2,1,0:T(8,128)(2,1)}, f32[64,64]{1,0:T(8,128)}) custom-call(s32[1]{0:T(128)} %bitcast.meta, f32[32,8,512]{2,1,0:T(8,128)} %copy-done.9, bf16[512,2048]{1,0:T(8,128)(2,1)} %acts_hbm.3, bf16[512,5120]{1,0:T(8,128)(2,1)} %cot_hbm.3, f32[64,5120]{1,0:T(8,128)} %bitcast.22), custom_call_target="tpu_custom_call" | custom-call | flops 49999998976 | bytes 1 | tf_op jit(solution)/shard_map/right/pallas_call | solution.py:42
  83.4 0.0 copy-start.4
  83.4 4.9 %all-to-all-start.3 = ((bf16[32,16,640]{2,1,0:T(8,128)(2,1)}), bf16[32,16,640]{2,1,0:T(8,128)(2,1)S(1)}, u32[]{:S(2)}, u32[]{:S(2)}) async-start(bf16[32,16,640]{2,1,0:T(8,128)(2,1)} %get-tuple-element.49), calls=%async_computation.3 | async-start | bytes 1310720 | tf_op jit(solution)/shard_map/all_to_all | solution.py:328
  88.2 0.0 collective-permute-done.5
  88.3 0.0 collective-permute-done.6
  88.3 0.0 collective-permute-done.4
  88.3 0.0 collective-permute-done.7
  88.3 0.0 copy-done.4
  88.3 2.2 %add_convert_fusion.1 = bf16[2,128,2560]{2,1,0:T(8,128)(2,1)S(1)} fusion(bf16[2,128,2560]{2,1,0:T(8,128)(2,1)} %collective-permute-done.5, bf16[2,128,2560]{2,1,0:T(8,128)(2,1)} %collective-permute-done.4, bf16[2,128,2560]{2,1,0:T(8,128)(2,1)S(1)} %copy-done.4), kind=kLoop, calls=%fused_computation.1 | loop fusion | flops 3932160 | bytes 5242880 | tf_op jit(solution)/shard_map/convert_element_type | solution.py:347
  90.5 0.0 copy-start.2
  90.5 0.0 copy-start.3
  90.6 1.0 copy-done.2
  91.5 1.4 collective-permute-start.8
  92.9 0.0 copy-done.3
  92.9 1.8 %add_convert_fusion = bf16[2,128,2560]{2,1,0:T(8,128)(2,1)S(1)} fusion(bf16[2,128,2560]{2,1,0:T(8,128)(2,1)} %collective-permute-done.7, bf16[2,128,2560]{2,1,0:T(8,128)(2,1)S(1)} %collective-permute-done.6, bf16[2,128,2560]{2,1,0:T(8,128)(2,1)S(1)} %copy-done.3), kind=kLoop, calls=%fused_computation | loop fusion | flops 3932160 | bytes 5242880 | tf_op jit(solution)/shard_map/convert_element_type | solution.py:347
  94.7 0.1 slice_bitcast_fusion
  94.8 2.1 %collective-permute-start.10 = (bf16[128,2560]{1,0:T(8,128)(2,1)S(1)}, bf16[128,2560]{1,0:T(8,128)(2,1)}, u32[]{:S(2)}, u32[]{:S(2)}) collective-permute-start(bf16[128,2560]{1,0:T(8,128)(2,1)S(1)} %get-tuple-element.71), channel_id=1, source_target_pairs={{0,6},{1,25},{2,0},{3,27},{4,2},{5,29},{6,4},{7,31},{8,14},{9,1},{... | collective-permute-start | bytes 1966088 | tf_op jit(solution)/shard_map/ppermute | solution.py:343
  96.9 1.0 collective-permute-start.9
  97.9 3.4 %all-to-all-done.3.part = bf16[32,16,640]{2,1,0:T(8,128)(2,1)S(1)} async-done(((bf16[32,16,640]{2,1,0:T(8,128)(2,1)}), bf16[32,16,640]{2,1,0:T(8,128)(2,1)S(1)}, u32[]{:S(2)}, u32[]{:S(2)}) %all-to-all-start.3) | async-done | bytes 655392 | tf_op jit(solution)/shard_map/all_to_all | solution.py:328
  101.3 0.8 right_shard.1
  102.0 8.2 %all-to-all-start.4 = ((bf16[8,16,640]{2,1,0:T(8,128)(2,1)}), bf16[8,16,640]{2,1,0:T(8,128)(2,1)S(1)}, u32[]{:S(2)}, u32[]{:S(2)}) async-start(bf16[8,16,640]{2,1,0:T(8,128)(2,1)} %right_shard.1), calls=%async_computation.4 | async-start | bytes 327680 | tf_op jit(solution)/shard_map/all_to_all | solution.py:328
  110.2 0.0 collective-permute-done.8
  110.2 1.2 collective-permute-done.10
  111.4 2.2 %collective-permute-done.9 = bf16[128,2560]{1,0:T(8,128)(2,1)} collective-permute-done((bf16[128,2560]{1,0:T(8,128)(2,1)S(1)}, bf16[128,2560]{1,0:T(8,128)(2,1)}, u32[]{:S(2)}, u32[]{:S(2)}) %collective-permute-start.9) | collective-permute-done | bytes 655392 | tf_op jit(solution)/shard_map/ppermute | solution.py:343
  113.6 6.8 %all-to-all-done.4.part = bf16[8,16,640]{2,1,0:T(8,128)(2,1)S(1)} async-done(((bf16[8,16,640]{2,1,0:T(8,128)(2,1)}), bf16[8,16,640]{2,1,0:T(8,128)(2,1)S(1)}, u32[]{:S(2)}, u32[]{:S(2)}) %all-to-all-start.4) | async-done | bytes 163872 | tf_op jit(solution)/shard_map/all_to_all | solution.py:328
  120.5 0.9 right_rep.1
  121.4 4.0 %all-to-all-start.5 = ((bf16[32,16,640]{2,1,0:T(8,128)(2,1)}), bf16[32,16,640]{2,1,0:T(8,128)(2,1)S(1)}, u32[]{:S(2)}, u32[]{:S(2)}) async-start(bf16[32,16,640]{2,1,0:T(8,128)(2,1)} %right_rep.1), calls=%async_computation.5 | async-start | bytes 1310720 | tf_op jit(solution)/shard_map/all_to_all | solution.py:328
  125.4 0.0 copy-start
  125.4 1.9 %fusion.2 = (bf16[64,2560]{1,0:T(8,128)(2,1)S(1)}, bf16[64,2560]{1,0:T(8,128)(2,1)S(1)}) fusion(bf16[2,128,2560]{2,1,0:T(8,128)(2,1)} %copy-done.2, bf16[128,2560]{1,0:T(8,128)(2,1)} %collective-permute-done.10, bf16[128,2560]{1,0:T(8,128)(2,1)} %collective-permute-done.9, bf16[128,2560]{1,0:T(8,128)(2,1)S(1)} %collective-permute-done.8), kind=kLoop, calls=%fused_computation.10 | loop fusion | flops 2621440 | bytes 3276800 | tf_op jit(solution)/shard_map/convert_element_type | solution.py:347
  127.3 0.4 collective-permute-start.11
  127.8 1.3 collective-permute-done.11.theirs
  129.0 9.4 %all-to-all-done.5.parts = bf16[32,16,640]{2,1,0:T(8,128)(2,1)S(1)} async-done(((bf16[32,16,640]{2,1,0:T(8,128)(2,1)}), bf16[32,16,640]{2,1,0:T(8,128)(2,1)S(1)}, u32[]{:S(2)}, u32[]{:S(2)}) %all-to-all-start.5) | async-done | bytes 655392 | tf_op jit(solution)/shard_map/all_to_all | solution.py:328
  138.5 2.2 %last.1 = (bf16[64,5120]{1,0:T(8,128)(2,1)}, f32[64,5120]{1,0:T(8,128)}, f32[64,5120]{1,0:T(8,128)}) custom-call(s32[1]{0:T(128)} %bitcast.meta, bf16[32,16,640]{2,1,0:T(8,128)(2,1)S(1)} %all-to-all-done.5.parts, f32[64,64]{1,0:T(8,128)S(1)} %copy-done.1, bf16[64,2560]{1,0:T(8,128)(2,1)S(1)} %get-tuple-element.70.mine, ...), custom_call_target="tpu_custom_call" | custom-call | flops 49999998976 | bytes 1 | tf_op jit(solution)/shard_map/last/pallas_call | solution.py:42
  (7 shorter events, 0.1 us)
Async XLA Ops:
  0.6 16.3 %collective-permute-start.1 = (bf16[512,5120]{1,0:T(8,128)(2,1)}, bf16[512,5120]{1,0:T(8,128)(2,1)}, u32[]{:S(2)}, u32[]{:S(2)}) collective-permute-start(bf16[512,5120]{1,0:T(8,128)(2,1)} %cot_hbm.3), channel_id=1, source_target_pairs={{0,1},{1,0},{2,3},{3,2},{4,5},{5,4},{6,7},{7,6},{8,9},{9,8},{10,11... | collective-permute-start | bytes 15728648 | tf_op jit(solution)/shard_map/ppermute | solution.py:364
  4.0 12.9 %collective-permute-start = (bf16[512,2048]{1,0:T(8,128)(2,1)}, bf16[512,2048]{1,0:T(8,128)(2,1)}, u32[]{:S(2)}, u32[]{:S(2)}) collective-permute-start(bf16[512,2048]{1,0:T(8,128)(2,1)} %acts_hbm.3), channel_id=1, source_target_pairs={{0,1},{1,0},{2,3},{3,2},{4,5},{5,4},{6,7},{7,6},{8,9},{9,8},{10,11... | collective-permute-start | bytes 6291464 | tf_op jit(solution)/shard_map/ppermute | solution.py:363
  11.1 21.9 %all-to-all-start = ((f32[32,8,512]{2,1,0:T(8,128)}), f32[32,8,512]{2,1,0:T(8,128)S(1)}, u32[]{:S(2)}, u32[]{:S(2)}) async-start(f32[32,8,512]{2,1,0:T(8,128)} %left.1), calls=%async_computation | async-start | bytes 1048576 | tf_op jit(solution)/shard_map/all_to_all | solution.py:328
  33.0 18.4 %collective-permute-start.2 = (bf16[2,128,2560]{2,1,0:T(8,128)(2,1)}, bf16[2,128,2560]{2,1,0:T(8,128)(2,1)}, u32[]{:S(2)}, u32[]{:S(2)}) collective-permute-start(bf16[2,128,2560]{2,1,0:T(8,128)(2,1)} %get-tuple-element.39), channel_id=1, source_target_pairs={{0,8},{1,3},{2,10},{3,5},{4,12},{5,7},{6,14},{7,1},{8,16},{9,11},{... | collective-permute-start | bytes 3932168 | tf_op jit(solution)/shard_map/ppermute | solution.py:343
  34.5 17.1 %collective-permute-start.3 = (bf16[2,128,2560]{2,1,0:T(8,128)(2,1)}, bf16[2,128,2560]{2,1,0:T(8,128)(2,1)S(1)}, u32[]{:S(2)}, u32[]{:S(2)}) collective-permute-start(bf16[2,128,2560]{2,1,0:T(8,128)(2,1)} %get-tuple-element.41), channel_id=1, source_target_pairs={{0,24},{1,7},{2,26},{3,1},{4,28},{5,3},{6,30},{7,5},{8,0},{9,15},{... | collective-permute-start | bytes 3932168 | tf_op jit(solution)/shard_map/ppermute | solution.py:343
  36.5 16.1 %all-to-all-start.1 = ((f32[8,8,512]{2,1,0:T(8,128)}), f32[8,8,512]{2,1,0:T(8,128)S(1)}, u32[]{:S(2)}, u32[]{:S(2)}) async-start(f32[8,8,512]{2,1,0:T(8,128)} %left_shard.1), calls=%async_computation.1 | async-start | bytes 262144 | tf_op jit(solution)/shard_map/all_to_all | solution.py:328
  44.7 43.5 %collective-permute-start.5 = (bf16[2,128,2560]{2,1,0:T(8,128)(2,1)}, bf16[2,128,2560]{2,1,0:T(8,128)(2,1)}, u32[]{:S(2)}, u32[]{:S(2)}) collective-permute-start(bf16[2,128,2560]{2,1,0:T(8,128)(2,1)} %get-tuple-element.52), channel_id=1, source_target_pairs={{0,24},{1,7},{2,26},{3,1},{4,28},{5,3},{6,30},{7,5},{8,0},{9,15},{... | collective-permute-start | bytes 3932168 | tf_op jit(solution)/shard_map/ppermute | solution.py:343
  46.1 42.2 %collective-permute-start.6 = (bf16[2,128,2560]{2,1,0:T(8,128)(2,1)}, bf16[2,128,2560]{2,1,0:T(8,128)(2,1)S(1)}, u32[]{:S(2)}, u32[]{:S(2)}) collective-permute-start(bf16[2,128,2560]{2,1,0:T(8,128)(2,1)} %get-tuple-element.54), channel_id=1, source_target_pairs={{0,8},{1,3},{2,10},{3,5},{4,12},{5,7},{6,14},{7,1},{8,16},{9,11},{... | collective-permute-start | bytes 3932168 | tf_op jit(solution)/shard_map/ppermute | solution.py:343
  51.6 1.1 copy-start.7
  52.6 9.1 %copy-start.6 = (bf16[2,128,2560]{2,1,0:T(8,128)(2,1)S(1)}, bf16[2,128,2560]{2,1,0:T(8,128)(2,1)}, u32[]{:S(2)}) copy-start(bf16[2,128,2560]{2,1,0:T(8,128)(2,1)} %get-tuple-element.44) | copy-start | bytes 3932164
  53.5 21.2 %all-to-all-start.2 = ((f32[32,8,512]{2,1,0:T(8,128)}), f32[32,8,512]{2,1,0:T(8,128)S(1)}, u32[]{:S(2)}, u32[]{:S(2)}) async-start(f32[32,8,512]{2,1,0:T(8,128)} %left_rep.1), calls=%async_computation.2 | async-start | bytes 1048576 | tf_op jit(solution)/shard_map/all_to_all | solution.py:328
  61.7 4.2 %copy-start.5 = (bf16[2,128,2560]{2,1,0:T(8,128)(2,1)S(1)}, bf16[2,128,2560]{2,1,0:T(8,128)(2,1)}, u32[]{:S(2)}) copy-start(bf16[2,128,2560]{2,1,0:T(8,128)(2,1)} %get-tuple-element.46) | copy-start | bytes 3932164
  61.7 4.2 %copy-start.8 = (bf16[2,128,2560]{2,1,0:T(8,128)(2,1)S(1)}, bf16[2,128,2560]{2,1,0:T(8,128)(2,1)}, u32[]{:S(2)}) copy-start(bf16[2,128,2560]{2,1,0:T(8,128)(2,1)} %copy-done.7) | copy-start | bytes 3932164
  64.6 23.7 %collective-permute-start.4 = (bf16[2,128,2560]{2,1,0:T(8,128)(2,1)}, bf16[2,128,2560]{2,1,0:T(8,128)(2,1)}, u32[]{:S(2)}, u32[]{:S(2)}) collective-permute-start(bf16[2,128,2560]{2,1,0:T(8,128)(2,1)} %add_convert_fusion.3), channel_id=1, source_target_pairs={{0,8},{1,3},{2,10},{3,5},{4,12},{5,7},{6,14},{7,1},{8,16},{9,11},{... | collective-permute-start | bytes 3932168 | tf_op jit(solution)/shard_map/ppermute | solution.py:343
  67.3 20.9 %collective-permute-start.7 = (bf16[2,128,2560]{2,1,0:T(8,128)(2,1)}, bf16[2,128,2560]{2,1,0:T(8,128)(2,1)}, u32[]{:S(2)}, u32[]{:S(2)}) collective-permute-start(bf16[2,128,2560]{2,1,0:T(8,128)(2,1)} %add_convert_fusion.2), channel_id=1, source_target_pairs={{0,24},{1,7},{2,26},{3,1},{4,28},{5,3},{6,30},{7,5},{8,0},{9,15},{... | collective-permute-start | bytes 3932168 | tf_op jit(solution)/shard_map/ppermute | solution.py:343
  74.7 0.8 copy-start.9
  83.4 4.9 %copy-start.4 = (bf16[2,128,2560]{2,1,0:T(8,128)(2,1)S(1)}, bf16[2,128,2560]{2,1,0:T(8,128)(2,1)}, u32[]{:S(2)}) copy-start(bf16[2,128,2560]{2,1,0:T(8,128)(2,1)} %get-tuple-element.50) | copy-start | bytes 3932164
  83.4 17.9 %all-to-all-start.3 = ((bf16[32,16,640]{2,1,0:T(8,128)(2,1)}), bf16[32,16,640]{2,1,0:T(8,128)(2,1)S(1)}, u32[]{:S(2)}, u32[]{:S(2)}) async-start(bf16[32,16,640]{2,1,0:T(8,128)(2,1)} %get-tuple-element.49), calls=%async_computation.3 | async-start | bytes 1310720 | tf_op jit(solution)/shard_map/all_to_all | solution.py:328
  90.5 1.1 copy-start.2
  90.5 2.4 %copy-start.3 = (bf16[2,128,2560]{2,1,0:T(8,128)(2,1)S(1)}, bf16[2,128,2560]{2,1,0:T(8,128)(2,1)}, u32[]{:S(2)}) copy-start(bf16[2,128,2560]{2,1,0:T(8,128)(2,1)} %get-tuple-element.37) | copy-start | bytes 3932164
  91.5 18.7 %collective-permute-start.8 = (bf16[128,2560]{1,0:T(8,128)(2,1)S(1)}, bf16[128,2560]{1,0:T(8,128)(2,1)S(1)}, u32[]{:S(2)}, u32[]{:S(2)}) collective-permute-start(bf16[128,2560]{1,0:T(8,128)(2,1)S(1)} %slice_bitcast_fusion.2), channel_id=1, source_target_pairs={{0,2},{1,9},{2,4},{3,11},{4,6},{5,13},{6,0},{7,15},{8,10},{9,17},{... | collective-permute-start | bytes 1966088 | tf_op jit(solution)/shard_map/ppermute | solution.py:343
  94.8 16.6 %collective-permute-start.10 = (bf16[128,2560]{1,0:T(8,128)(2,1)S(1)}, bf16[128,2560]{1,0:T(8,128)(2,1)}, u32[]{:S(2)}, u32[]{:S(2)}) collective-permute-start(bf16[128,2560]{1,0:T(8,128)(2,1)S(1)} %get-tuple-element.71), channel_id=1, source_target_pairs={{0,6},{1,25},{2,0},{3,27},{4,2},{5,29},{6,4},{7,31},{8,14},{9,1},{... | collective-permute-start | bytes 1966088 | tf_op jit(solution)/shard_map/ppermute | solution.py:343
  96.9 16.8 %collective-permute-start.9 = (bf16[128,2560]{1,0:T(8,128)(2,1)S(1)}, bf16[128,2560]{1,0:T(8,128)(2,1)}, u32[]{:S(2)}, u32[]{:S(2)}) collective-permute-start(bf16[128,2560]{1,0:T(8,128)(2,1)S(1)} %get-tuple-element.72), channel_id=1, source_target_pairs={{0,4},{1,17},{2,6},{3,19},{4,0},{5,21},{6,2},{7,23},{8,12},{9,25},... | collective-permute-start | bytes 1966088 | tf_op jit(solution)/shard_map/ppermute | solution.py:343
  102.0 18.4 %all-to-all-start.4 = ((bf16[8,16,640]{2,1,0:T(8,128)(2,1)}), bf16[8,16,640]{2,1,0:T(8,128)(2,1)S(1)}, u32[]{:S(2)}, u32[]{:S(2)}) async-start(bf16[8,16,640]{2,1,0:T(8,128)(2,1)} %right_shard.1), calls=%async_computation.4 | async-start | bytes 327680 | tf_op jit(solution)/shard_map/all_to_all | solution.py:328
  121.4 17.1 %all-to-all-start.5 = ((bf16[32,16,640]{2,1,0:T(8,128)(2,1)}), bf16[32,16,640]{2,1,0:T(8,128)(2,1)S(1)}, u32[]{:S(2)}, u32[]{:S(2)}) async-start(bf16[32,16,640]{2,1,0:T(8,128)(2,1)} %right_rep.1), calls=%async_computation.5 | async-start | bytes 1310720 | tf_op jit(solution)/shard_map/all_to_all | solution.py:328
  125.4 13.1 %copy-start = (f32[1,64,5120]{2,1,0:T(8,128)S(1)}, f32[1,64,5120]{2,1,0:T(8,128)}, u32[]{:S(2)}) copy-start(f32[1,64,5120]{2,1,0:T(8,128)} %param.6) | copy-start | bytes 3932164
  125.4 13.0 %copy-start.1 = (f32[64,64]{1,0:T(8,128)S(1)}, f32[64,64]{1,0:T(8,128)}, u32[]{:S(2)}) copy-start(f32[64,64]{1,0:T(8,128)} %get-tuple-element.62.own_t) | copy-start | bytes 49156
  127.3 1.7 %collective-permute-start.11 = (bf16[64,2560]{1,0:T(8,128)(2,1)S(1)}, bf16[64,2560]{1,0:T(8,128)(2,1)S(1)}, u32[]{:S(2)}, u32[]{:S(2)}) collective-permute-start(bf16[64,2560]{1,0:T(8,128)(2,1)S(1)} %get-tuple-element.69), channel_id=1, source_target_pairs={{0,1},{1,0},{2,3},{3,2},{4,5},{5,4},{6,7},{7,6},{8,9},{9,8},{10,11... | collective-permute-start | bytes 983048 | tf_op jit(solution)/shard_map/ppermute | solution.py:405
